TPU v7x, 256 devices: a whole 4x4x8 slice. The times are simulated.
256 devices in a mesh: rows: 16 (over z_lo, x, core), rep: 16 (over y, z_hi).
Axes of the slice: x: 4, y: 4, z: 8 (z_hi: 4, z_lo: 2; z = z_hi * 2 + z_lo), core: 2. Of those that a mesh axis runs over, the one named last changes fastest.
Arguments:
- node_features: bfloat16 [32768, 256], P(('rows', 'rep')), may hold values from -6 to 6
- adjacency: bfloat16 [256, 64, 128, 128], P('rows', 'rep'), may hold values from -0.078125 to 0.078125
- column_ids: int32 [256, 64], P('rows', 'rep'), may hold values from 0 to 15
- block_counts: int32 [256, 16], P('rows', 'rep'), may hold values from 1 to 4, 40 in all within a row
- weight_first: bfloat16 [256, 512], replicated, may hold values from -0.375 to 0.375
- weight_second: bfloat16 [512, 256], replicated, may hold values from -0.25 to 0.25
- cotangent: bfloat16 [32768, 256], P(('rows', 'rep')), may hold values from -6 to 6
Outputs:
- embedding: bfloat16 [32768, 256], P(('rows', 'rep'))
- grad_first: float32 [256, 512], replicated
- grad_second: float32 [512, 256], replicated
Inputs may be any that keep to these rules, and one draw needn't show every extreme that they name: `block_counts`: each row block has 40 live slots over its 16 groups; some group of some row block has all 4 live.
All inputs are finite; a program needn't handle non-finite values.
Results may differ from a plain program's by a relative error of at most 0.024.
Values may be sent and summed in bfloat16 or wider, within the bound.
A program may use at most 64 MiB of HBM per device.

v0:
```python
import math

import jax
import jax.numpy as jnp
from jax import lax
from jax.sharding import PartitionSpec as P

BS = 128


def slot_weights(adjacency, block_counts, slot):
    weights = adjacency[:, slot]
    live_rows = slot < block_counts[:, 0]
    return jnp.where(live_rows[:, None, None], weights, jnp.zeros_like(weights))


def aggregate(node_field, adjacency, column_ids, block_counts):
    feature_width = node_field.shape[1]
    gathered = lax.all_gather(node_field, "rows", axis=0, tiled=True)
    blocks_in = gathered.reshape(-1, BS, feature_width)
    row_blocks = column_ids.shape[0]
    partial_sum = jnp.zeros((row_blocks, BS, feature_width), jnp.float32)
    for slot in range(column_ids.shape[1]):
        weights = slot_weights(adjacency, block_counts, slot)
        picked = blocks_in[column_ids[:, slot]]
        partial_sum = partial_sum + jnp.einsum(
            "rij,rjf->rif", weights, picked, preferred_element_type=jnp.float32
        )
    return lax.psum_scatter(
        partial_sum.reshape(row_blocks * BS, feature_width).astype(jnp.bfloat16),
        "rep",
        scatter_dimension=0,
        tiled=True,
    ).astype(jnp.float32)


def transpose_aggregate(cotangent, adjacency, column_ids, block_counts):
    feature_width = cotangent.shape[1]
    row_blocks = column_ids.shape[0]
    gathered = lax.all_gather(cotangent, "rep", axis=0, tiled=True).reshape(
        row_blocks, BS, feature_width
    )
    col_blocks = lax.axis_size("rows") * (cotangent.shape[0] // BS)
    summed = jnp.zeros((col_blocks, BS, feature_width), jnp.float32)
    for slot in range(column_ids.shape[1]):
        weights = slot_weights(adjacency, block_counts, slot)
        terms = jnp.einsum("rij,rif->rjf", weights, gathered, preferred_element_type=jnp.float32)
        summed = summed.at[column_ids[:, slot]].add(terms)
    return lax.psum_scatter(
        summed.reshape(col_blocks * BS, feature_width).astype(jnp.bfloat16),
        "rows",
        scatter_dimension=0,
        tiled=True,
    ).astype(jnp.float32)


def shards(
    node_features, adjacency, column_ids, block_counts, weight_first, weight_second, cotangent
):
    contract = (((0,), (0,)), ((), ()))
    mixed_input = aggregate(node_features, adjacency, column_ids, block_counts).astype(jnp.bfloat16)
    pre_first = jnp.dot(mixed_input, weight_first, preferred_element_type=jnp.float32)
    hidden = jax.nn.silu(pre_first).astype(jnp.bfloat16)
    second_in = jnp.dot(hidden, weight_second, preferred_element_type=jnp.float32).astype(
        jnp.bfloat16
    )
    embedding = aggregate(second_in, adjacency, column_ids, block_counts).astype(jnp.bfloat16)
    upstream = transpose_aggregate(cotangent, adjacency, column_ids, block_counts).astype(
        jnp.bfloat16
    )
    node_total = node_features.shape[0] * lax.axis_size("rows") * lax.axis_size("rep")
    scale_factor = 1.0 / math.sqrt(node_total)
    local_second = lax.dot_general(hidden, upstream, contract, preferred_element_type=jnp.float32)
    back_hidden = lax.dot_general(
        upstream, weight_second, (((1,), (1,)), ((), ())), preferred_element_type=jnp.float32
    )
    sigmoid_gate = jax.nn.sigmoid(pre_first)
    back_pre = (back_hidden * sigmoid_gate * (1.0 + pre_first * (1.0 - sigmoid_gate))).astype(
        jnp.bfloat16
    )
    local_first = lax.dot_general(
        mixed_input, back_pre, contract, preferred_element_type=jnp.float32
    )
    grad_first, grad_second = lax.psum((local_first, local_second), ("rows", "rep"))
    return (embedding, grad_first * scale_factor, grad_second * scale_factor)


def solution(mesh):
    in_specs = (
        P(("rows", "rep"), None),
        P("rows", "rep", None, None),
        P("rows", "rep"),
        P("rows", "rep"),
        P(),
        P(),
        P(("rows", "rep"), None),
    )
    out_specs = (P(("rows", "rep"), None), P(), P())
    return jax.shard_map(shards, mesh=mesh, in_specs=in_specs, out_specs=out_specs, check_vma=False)
```

profile of v0, /device:TPU:1, one launch (start us, length us, event | category | flops | bytes accessed | tf_op | source)
XLA Modules:
  0.0 648.5 jit_solution(16340234801673374021)
XLA Ops:
  10.2 38.9 %all-gather.4.cloned.1.call-done = bf16[2048,256]{1,0:T(8,128)(2,1)} async-done(((bf16[128,256]{1,0:T(8,128)(2,1)}), bf16[2048,256]{1,0:T(8,128)(2,1)}) %all-gather.4.cloned.1.call-update) | async-done | bytes 1048592 | tf_op jit(solution)/shard_map/all_gather | solution.py:19
  49.1 2.9 gather_fusion.2
  52.0 1.6 gather_fusion
  53.6 1.6 gather_fusion.1
  55.2 1.6 gather_fusion.3
  56.8 1.8 fusion.21
  62.1 41.4 %all-gather.8.cloned.1.call-done = bf16[2048,256]{1,0:T(8,128)(2,1)} async-done(((bf16[128,256]{1,0:T(8,128)(2,1)}), bf16[2048,256]{1,0:T(8,128)(2,1)}) %all-gather.8.cloned.1.call-update) | async-done | bytes 1048592 | tf_op jit(solution)/shard_map/all_gather | solution.py:40
  103.6 3.3 fusion.16
  107.1 3.5 scatter_fusion
  110.6 3.1 fusion.13
  113.7 3.5 scatter_fusion.1
  117.2 3.1 fusion.19
  120.4 3.5 scatter_fusion.2
  123.9 3.1 fusion.22
  127.0 3.5 scatter_fusion.3
  131.7 58.3 %reduce-scatter.4.cloned.1.call-done = bf16[128,256]{1,0:T(8,128)(2,1)} async-done(((bf16[2048,256]{1,0:T(8,128)(2,1)}), bf16[128,256]{1,0:T(8,128)(2,1)}) %reduce-scatter.4.cloned.1.call-update) | async-done | bytes 65552 | tf_op jit(solution)/shard_map/reduce_scatter | solution.py:29
  192.1 60.9 %reduce-scatter.8.cloned.1.call-done = bf16[128,256]{1,0:T(8,128)(2,1)} async-done(((bf16[2048,256]{1,0:T(8,128)(2,1)}), bf16[128,256]{1,0:T(8,128)(2,1)}) %reduce-scatter.8.cloned.1.call-update) | async-done | bytes 65552 | tf_op jit(solution)/shard_map/reduce_scatter | solution.py:49
  252.9 1.9 fusion.12
  254.9 2.1 fusion.2
  257.0 35.0 %all-gather.6.cloned.1.call-done = bf16[2048,256]{1,0:T(8,128)(2,1)} async-done(((bf16[128,256]{1,0:T(8,128)(2,1)}), bf16[2048,256]{1,0:T(8,128)(2,1)}) %all-gather.6.cloned.1.call-update) | async-done | bytes 1048592 | tf_op jit(solution)/shard_map/all_gather | solution.py:19
  291.9 2.9 gather_fusion.6
  294.8 1.6 gather_fusion.4
  296.5 1.6 gather_fusion.5
  298.1 3.1 fusion.20
  301.2 1.8 fusion.17
  303.0 1.8 fusion.14
  304.9 1.7 gather_fusion.7
  306.5 4.8 add_convert_fusion
  311.3 241.1 %all-reduce.3.cloned.1.call-done = (f32[256,512]{1,0:T(8,128)}, f32[512,256]{1,0:T(8,128)}) async-done(((f32[256,512]{1,0:T(8,128)}, f32[512,256]{1,0:T(8,128)}), (f32[256,512]{1,0:T(8,128)}, f32[512,256]{1,0:T(8,128)})) %all-reduce.3.cloned.1.call-update) | async-done | bytes 1048592 | tf_op jit(solution)/shard_map/psum | solution.py:84
  552.4 1.9 broadcast_multiply_fusion.1
  554.3 1.9 broadcast_multiply_fusion
  556.2 85.4 %reduce-scatter.6.cloned.1.call-done = bf16[128,256]{1,0:T(8,128)(2,1)} async-done(((bf16[2048,256]{1,0:T(8,128)(2,1)}), bf16[128,256]{1,0:T(8,128)(2,1)}) %reduce-scatter.6.cloned.1.call-update) | async-done | bytes 65552 | tf_op jit(solution)/shard_map/reduce_scatter | solution.py:29
  (51 shorter events, 9.9 us)
Async XLA Ops:
  7.2 184.0 %copy-start = (bf16[512,256]{1,0:T(8,128)(2,1)S(1)}, bf16[512,256]{1,0:T(8,128)(2,1)}, u32[]{:S(2)}) copy-start(bf16[512,256]{1,0:T(8,128)(2,1)} %param.12) | copy-start | bytes 786436
  7.2 41.9 %all-gather.4.cloned.1.call-start = ((), (), s32[]{:S(2)}) async-start(), calls=%async_computation.3 | async-start | bytes 1114112 | tf_op jit(solution)/shard_map/all_gather | solution.py:19
  7.9 95.6 %all-gather.8.cloned.1.call-start = ((), (), s32[]{:S(2)}) async-start(), calls=%async_computation.7 | async-start | bytes 1114112 | tf_op jit(solution)/shard_map/all_gather | solution.py:40
  8.7 181.4 %reduce-scatter.4.cloned.1.call-start = ((), (), s32[]{:S(2)}) async-start(), calls=%async_computation.4 | async-start | bytes 1114112 | tf_op jit(solution)/shard_map/reduce_scatter | solution.py:29
  49.1 2.9 copy-start.4
  53.6 3.2 copy-start.1
  56.8 1.8 copy-start.8
  58.6 1.2 copy-start.9
  59.2 1.3 copy-start.6
  62.1 190.9 %reduce-scatter.8.cloned.1.call-start = ((), (), s32[]{:S(2)}) async-start(), calls=%async_computation.8 | async-start | bytes 1114112 | tf_op jit(solution)/shard_map/reduce_scatter | solution.py:49
  107.1 3.5 copy-start.5
  130.5 59.5 %copy-start.11 = (bf16[256,512]{1,0:T(8,128)(2,1)S(1)}, bf16[256,512]{1,0:T(8,128)(2,1)}, u32[]{:S(2)}) copy-start(bf16[256,512]{1,0:T(8,128)(2,1)} %param.11) | copy-start | bytes 786436
  131.7 160.3 %all-gather.6.cloned.1.call-start = ((), (), s32[]{:S(2)}) async-start(), calls=%async_computation.5 | async-start | bytes 1114112 | tf_op jit(solution)/shard_map/all_gather | solution.py:19
  190.0 64.8 %copy-start.12 = (bf16[128,256]{1,0:T(8,128)(2,1)S(1)}, bf16[128,256]{1,0:T(8,128)(2,1)}, u32[]{:S(2)}) copy-start(bf16[128,256]{1,0:T(8,128)(2,1)} %reduce-scatter.4.cloned.1.call-done) | copy-start | bytes 196612
  192.0 360.4 %all-reduce.3.cloned.1.call-start = ((), (), s32[]{:S(2)}) async-start(), calls=%async_computation.9 | async-start | bytes 2097152 | tf_op jit(solution)/shard_map/psum | solution.py:84
  256.9 384.7 %reduce-scatter.6.cloned.1.call-start = ((), (), s32[]{:S(2)}) async-start(), calls=%async_computation.6 | async-start | bytes 1114112 | tf_op jit(solution)/shard_map/reduce_scatter | solution.py:29
  291.9 2.9 copy-start.3
  294.8 3.2 copy-start.2
  298.1 3.1 copy-start.10
  301.2 1.8 copy-start.7
Sparse Core Ops, SparseCore 0:
  9.9 39.1 all-gather.3
  51.5 51.9 all-gather.7
  107.1 82.9 reduce-scatter.3
  192.6 60.3 reduce-scatter.7
  255.2 36.6 all-gather.5
  298.0 254.3 all-reduce.2
  556.9 84.6 reduce-scatter.5
where the time goes:
time: 650 us; the launch traced here: 648 us
  waiting for transfers between devices  562 us (86%)
  matrix products  34.5 us (5%)
  other arithmetic  20.4 us (3%)
  local copies, waits for them, and re-layouts  16.5 us (3%)
  between operations  14.3 us (2%)
    psum x1, waiting for transfers between devices, shards(): lax.psum((local_first, local_second), ('rows', 'rep'))  241 us
    reduce_scatter x2, waiting for transfers between devices, aggregate(): lax.psum_scatter(partial_sum.reshape(row_blocks * BS, feature_width).asty...  144 us
    all_gather x2, waiting for transfers between devices, aggregate(): gathered = lax.all_gather(node_field, 'rows', axis=0, tiled=True)  73.8 us
    reduce_scatter x1, waiting for transfers between devices, transpose_aggregate(): lax.psum_scatter(summed.reshape(col_blocks * BS, feature_width).astype(jn...  60.9 us
    all_gather x1, waiting for transfers between devices, transpose_aggregate(): lax.all_gather(cotangent, 'rep', axis=0, tiled=True)  41.4 us
    dot_general x8, matrix products, aggregate(): jnp.einsum('rij,rjf->rif', weights, picked, preferred_element_type=jnp.fl...  15.9 us
    gather x8, local copies, waits for them, and re-layouts, aggregate(): picked = blocks_in[column_ids[:, slot]]  15.5 us
    scatter-add x4, other arithmetic, transpose_aggregate(): summed = summed.at[column_ids[:, slot]].add(terms)  14 us
  transfers between devices with their start and end apart: 7, of which 7 were waited for; matrix products, arithmetic and copies ran while one was open for 11% of the time, Pallas kernels for 0%

commit v1 on v0

v1 whole, which is shorter than its diff:
```python
import functools
import math

import jax
import jax.numpy as jnp
from jax import lax
from jax.experimental import pallas as pl
from jax.experimental.pallas import tpu as pltpu
from jax.sharding import PartitionSpec as P

MESH = pl.DeviceIdType.MESH
F32 = jnp.float32
BF16 = jnp.bfloat16
NY = 4


def dot(a, b):
    return jnp.dot(a, b, preferred_element_type=F32)


def dot_dims(a, b, ca, cb):
    return lax.dot_general(a, b, (((ca,), (cb,)), ((), ())), preferred_element_type=F32)


def loop(lo, hi, body):
    def step(i, carry):
        body(i)
        return carry

    lax.fori_loop(lo, hi, step, 0)


def kernel(
    ny,
    scale,
    ids,
    counts,
    x_ref,
    adj_ref,
    w1_ref,
    w2_ref,
    cot_ref,
    emb_ref,
    g1_ref,
    g2_ref,
    dense,
    feat1,
    feat2,
    cotb,
    terms1,
    terms2,
    ybuf1,
    ybuf2,
    zsend1,
    zsend2,
    zrecv1,
    zrecv2,
    own_sum,
    second,
    tsend,
    trecv,
    town,
    tchip,
    mixed_s,
    hidden_s,
    pre_s,
    glocal,
    gsib,
    gchip,
    gchip_r,
    gtile,
    gtile_r,
    gall,
    gfin,
    gpiece,
    s_ag1,
    r_ag1,
    f_ag1,
    s_ag2,
    r_ag2,
    f_ag2,
    s_ag3,
    r_ag3,
    f_ag3,
    s_cot,
    rz_cot,
    ry_cot,
    s_rs1,
    ry_rs1,
    rz_rs1,
    s_rs2,
    ry_rs2,
    rz_rs2,
    s_t,
    rs_t,
    rc_t,
    s_g,
    rs_g,
    rc_g,
    rr_g,
    ra_g,
):
    rows = lax.axis_size("rows")
    rep = lax.axis_size("rep")
    nq = rows // 2
    nz = rep // ny
    bs = x_ref.shape[0]
    r = lax.axis_index("rows")
    c = lax.axis_index("rep")
    core = lax.rem(r, 2)
    q = r // 2
    y = c // nz
    z = lax.rem(c, nz)
    sib = r + 1 - 2 * core

    def chip_at(d):
        return lax.rem(q + d, nq)

    def chip_before(d):
        return lax.rem(q + nq - d, nq)

    def at_chip(q2):
        return (2 * q2 + core, c)

    def at_y(dy):
        y2 = lax.rem(y + dy, ny)
        return y2, (r, y2 * nz + z)

    def at_z(dz):
        z2 = lax.rem(z + dz, nz)
        return z2, (r, y * nz + z2)

    def send(src, dst, ssem, rsem, dev):
        pltpu.make_async_remote_copy(
            src_ref=src, dst_ref=dst, send_sem=ssem, recv_sem=rsem, device_id=dev, device_id_type=MESH
        ).start()

    def wait(ref, sem):
        pltpu.make_async_copy(ref, ref, sem).wait()

    barrier = pltpu.get_barrier_semaphore()
    pl.semaphore_signal(barrier, inc=1, device_id=(sib, c), device_id_type=MESH)
    loop(1, nq, lambda d: pl.semaphore_signal(barrier, inc=1, device_id=at_chip(chip_at(d)), device_id_type=MESH))
    loop(
        1,
        rep,
        lambda d: pl.semaphore_signal(
            barrier, inc=1, device_id=(r, lax.rem(c + d, rep)), device_id_type=MESH
        ),
    )
    pl.semaphore_wait(barrier, 1 + (nq - 1) + (rep - 1))

    def gather_start(src, buf, ssem, rsem, fsem):
        loop(1, nq, lambda d: send(src, buf.at[core, q], ssem.at[0], rsem.at[d - 1], at_chip(chip_at(d))))
        send(src, buf.at[core, q], ssem.at[0], fsem.at[0], (sib, c))

    def gather_pass(buf, ssem, rsem, fsem):
        def one(d):
            block = buf.at[core, chip_before(d)]
            wait(block, rsem.at[d - 1])
            send(block, block, ssem.at[1], fsem.at[0], (sib, c))

        loop(1, nq, one)

    def gather_end(buf, ssem, fsem):
        wait(buf.at[1 - core], fsem.at[0])

    def gather_sent(buf, ssem):
        wait(buf.at[0], ssem.at[0])
        wait(buf.at[0, pl.ds(0, nq - 1)], ssem.at[1])

    gather_start(x_ref, feat1, s_ag1, r_ag1, f_ag1)
    feat1[core, q] = x_ref[...]

    cotb[z, y] = cot_ref[...].astype(F32).T.astype(BF16)
    own_cot = cotb.at[z, y]
    for dz in range(1, nz):
        send(own_cot, own_cot, s_cot.at[0], rz_cot.at[dz - 1], at_z(dz)[1])
    for dy in range(1, ny):
        send(own_cot, own_cot, s_cot.at[1], ry_cot.at[0], at_y(dy)[1])

    def densify(b):
        z2 = lax.rem(b, nz)
        y2 = b // nz
        blocks = [adj_ref[b, s] for s in range(adj_ref.shape[1])]
        zero = jnp.zeros_like(blocks[0])
        where_to = [jnp.where(s < counts[b, 0], ids[b, s], -1) for s in range(len(blocks))]
        row = pl.ds(pl.multiple_of(y2 * bs, bs), bs)
        for p in range(rows):
            total = jnp.where(where_to[0] == p, blocks[0], zero)
            for s in range(1, len(blocks)):
                total = total + jnp.where(where_to[s] == p, blocks[s], zero)
            dense[p % 2, z2, row, (p // 2) * bs : (p // 2 + 1) * bs] = total

    loop(0, rep, densify)

    gather_pass(feat1, s_ag1, r_ag1, f_ag1)
    for dz in range(1, nz):
        z3 = lax.rem(z + nz - dz, nz)
        block = cotb.at[z3, y]
        wait(block, rz_cot.at[dz - 1])
        for dy in range(1, ny):
            send(block, block, s_cot.at[1], ry_cot.at[dz], at_y(dy)[1])
    gather_end(feat1, s_ag1, f_ag1)

    def aggregate_start(feat, terms, ybuf, ssem, rysem):
        def one(k):
            z2 = lax.rem(z + k + 1, nz)
            total = dot(dense[0, z2], feat[0].reshape(nq * bs, -1))
            total = total + dot(dense[1, z2], feat[1].reshape(nq * bs, -1))
            terms[z2] = total.astype(BF16).reshape(terms.shape[1:])
            for dy in range(1, ny):
                y2, dev = at_y(dy)
                send(terms.at[z2, y2], ybuf.at[k, dy - 1], ssem.at[0], rysem.at[k], dev)

        loop(0, nz, one)

    def aggregate_fold(k, terms, ybuf, zsend, zrecv, ssem, rysem, rzsem):
        z2, dev = at_z(k + 1)
        wait(ybuf.at[k], rysem.at[k])
        total = terms[z2, y].astype(F32)
        for i in range(ny - 1):
            total = total + ybuf[k, i].astype(F32)
        if k < nz - 1:
            zsend[k] = total.astype(BF16)
            send(zsend.at[k], zrecv.at[k], ssem.at[1], rzsem.at[0], dev)
        else:
            own_sum[...] = total

    def aggregate_end(zrecv, rzsem):
        wait(zrecv, rzsem.at[0])
        total = own_sum[...]
        for k in range(nz - 1):
            total = total + zrecv[k].astype(F32)
        return total

    def aggregate_sent(ybuf, zsend, ssem):
        wait(ybuf, ssem.at[0])
        wait(zsend, ssem.at[1])

    aggregate_start(feat1, terms1, ybuf1, s_rs1, ry_rs1)

    for k in range(nz):
        wait(ybuf1.at[0], ry_cot.at[k])

    two = 2 * bs

    def transposed_terms(par, n):
        col = pl.ds(pl.multiple_of(n * two, two), two)
        total = None
        for z2 in range(nz):
            left = jnp.concatenate([cotb[z2, y2] for y2 in range(ny)], axis=1)
            part = dot(left, dense[par, z2, :, col])
            total = part if total is None else total + part
        return total

    def t_other(n):
        total = transposed_terms(1 - core, n).astype(BF16)
        tsend[2 * n] = total[:, :bs]
        tsend[2 * n + 1] = total[:, bs:]
        pair = pl.ds(2 * n, 2)
        send(tsend.at[pair], trecv.at[pair], s_t.at[0], rs_t.at[n], (sib, c))

    loop(0, nq // 2, t_other)

    fold1 = functools.partial(
        aggregate_fold,
        terms=terms1,
        ybuf=ybuf1,
        zsend=zsend1,
        zrecv=zrecv1,
        ssem=s_rs1,
        rysem=ry_rs1,
        rzsem=rz_rs1,
    )
    fold1(0)

    def t_own(n):
        total = transposed_terms(core, n)
        wait(trecv.at[pl.ds(2 * n, 2)], rs_t.at[n])
        town[2 * n] = (total[:, :bs] + trecv[2 * n].astype(F32)).astype(BF16)
        town[2 * n + 1] = (total[:, bs:] + trecv[2 * n + 1].astype(F32)).astype(BF16)

    loop(0, nq // 2, t_own)
    fold1(1)
    loop(
        1,
        nq,
        lambda d: send(town.at[chip_at(d)], tchip.at[d - 1], s_t.at[1], rc_t.at[0], at_chip(chip_at(d))),
    )
    for k in range(2, nz):
        fold1(k)

    mixed = aggregate_end(zrecv1, rz_rs1).astype(BF16)
    mixed_s[...] = mixed
    pre = dot(mixed, w1_ref[...])
    pre_s[...] = pre
    hidden = (pre / (1.0 + jnp.exp(-pre))).astype(BF16)
    hidden_s[...] = hidden
    second[...] = dot(hidden, w2_ref[...]).astype(BF16)
    gather_start(second, feat2, s_ag2, r_ag2, f_ag2)
    feat2[core, q] = second[...]

    wait(tchip, rc_t.at[0])
    up = town[q].astype(F32)
    for d in range(nq - 1):
        up = up + tchip[d].astype(F32)
    up_t = up.astype(BF16)
    glocal[1] = (dot(up_t, hidden_s[...]) * scale).astype(BF16)
    back = dot_dims(up.T.astype(BF16), w2_ref[...], 1, 1)
    pre = pre_s[...]
    gate = 1.0 / (1.0 + jnp.exp(-pre))
    back_pre = (back * gate * (1.0 + pre * (1.0 - gate))).astype(BF16)
    glocal[0] = (dot_dims(mixed_s[...], back_pre, 0, 0) * scale).astype(BF16)
    send(glocal.at[1 - core], gsib, s_g.at[0], rs_g.at[0], (sib, c))

    gather_pass(feat2, s_ag2, r_ag2, f_ag2)

    wait(gsib, rs_g.at[0])
    gchip[...] = (glocal[core].astype(F32) + gsib[...].astype(F32)).astype(BF16).reshape(gchip.shape)
    loop(
        1,
        nq,
        lambda d: send(gchip.at[chip_at(d)], gchip_r.at[d - 1], s_g.at[1], rc_g.at[0], at_chip(chip_at(d))),
    )

    gather_end(feat2, s_ag2, f_ag2)
    aggregate_start(feat2, terms2, ybuf2, s_rs2, ry_rs2)
    fold2 = functools.partial(
        aggregate_fold,
        terms=terms2,
        ybuf=ybuf2,
        zsend=zsend2,
        zrecv=zrecv2,
        ssem=s_rs2,
        rysem=ry_rs2,
        rzsem=rz_rs2,
    )

    wait(gchip_r, rc_g.at[0])
    share = gchip[q].astype(F32)
    for d in range(nq - 1):
        share = share + gchip_r[d].astype(F32)
    tile_rows, tile_cols = gtile.shape[1:]
    across = share.shape[1] // tile_cols
    for t in range(rep):
        i, j = t // across, t % across
        gtile[t] = share[i * tile_rows : (i + 1) * tile_rows, j * tile_cols : (j + 1) * tile_cols]

    def at_rep(d):
        return lax.rem(c + d, rep)

    loop(1, rep, lambda d: send(gtile.at[at_rep(d)], gtile_r.at[d - 1], s_g.at[2], rr_g.at[0], (r, at_rep(d))))

    fold2(0)

    wait(gtile_r, rr_g.at[0])
    tile = gtile[c]
    for d in range(rep - 1):
        tile = tile + gtile_r[d]
    gall[c] = tile
    loop(1, rep, lambda d: send(gall.at[c], gall.at[c], s_g.at[3], ra_g.at[0], (r, at_rep(d))))

    fold2(1)

    wait(gtile_r, ra_g.at[0])
    for i in range(rep // across):
        strip = jnp.concatenate([gall[i * across + j] for j in range(across)], axis=1)
        gpiece[i * tile_rows : (i + 1) * tile_rows, :] = strip
    gfin[core, q] = gpiece[...].astype(BF16)
    own_piece = gfin.at[core, q]
    gather_start(own_piece, gfin, s_ag3, r_ag3, f_ag3)

    for k in range(2, nz):
        fold2(k)
    gather_pass(gfin, s_ag3, r_ag3, f_ag3)
    emb_ref[...] = aggregate_end(zrecv2, rz_rs2).astype(BF16)

    gather_end(gfin, s_ag3, f_ag3)
    g1_ref[...] = gfin[0].reshape(g1_ref.shape).astype(F32)
    g2_ref[...] = gfin[1].reshape(g2_ref.shape[::-1]).astype(F32).T

    gather_sent(feat1, s_ag1)
    gather_sent(feat2, s_ag2)
    gather_sent(gfin, s_ag3)
    wait(cotb.at[0, pl.ds(0, nz - 1)], s_cot.at[0])
    wait(terms1.at[:, pl.ds(0, ny - 1)], s_cot.at[1])
    aggregate_sent(ybuf1, zsend1, s_rs1)
    aggregate_sent(ybuf2, zsend2, s_rs2)
    wait(tsend, s_t.at[0])
    wait(tchip, s_t.at[1])
    wait(gsib, s_g.at[0])
    wait(gchip_r, s_g.at[1])
    wait(gtile_r, s_g.at[2])
    wait(gtile_r, s_g.at[3])


def shards(ny, nodes, node_features, adjacency, column_ids, block_counts, w1, w2, cotangent):
    rows, rep = lax.axis_size("rows"), lax.axis_size("rep")
    nq, nz = rows // 2, rep // ny
    bs, width = node_features.shape
    hid = w1.shape[1]
    block = (bs, width)
    turned = (width, bs)
    share = (width // nq, hid)
    tile = (8, 128)
    vmem = pl.BlockSpec(memory_space=pltpu.VMEM)
    smem = pl.BlockSpec(memory_space=pltpu.SMEM)
    v = pltpu.VMEM
    dma = pltpu.SemaphoreType.DMA
    scratch = [
        v((2, nz, ny * bs, nq * bs), BF16),
        v((2, nq) + block, BF16),
        v((2, nq) + block, BF16),
        v((nz, ny) + turned, BF16),
        v((nz, ny) + block, BF16),
        v((nz, ny) + block, BF16),
        v((nz, ny - 1) + block, BF16),
        v((nz, ny - 1) + block, BF16),
        v((nz - 1,) + block, BF16),
        v((nz - 1,) + block, BF16),
        v((nz - 1,) + block, BF16),
        v((nz - 1,) + block, BF16),
        v(block, F32),
        v(block, BF16),
        v((nq,) + turned, BF16),
        v((nq,) + turned, BF16),
        v((nq,) + turned, BF16),
        v((nq - 1,) + turned, BF16),
        v(block, BF16),
        v((bs, hid), BF16),
        v((bs, hid), F32),
        v((2, width, hid), BF16),
        v((width, hid), BF16),
        v((nq,) + share, BF16),
        v((nq - 1,) + share, BF16),
        v((rep,) + tile, F32),
        v((rep - 1,) + tile, F32),
        v((rep,) + tile, F32),
        v((2, nq) + share, BF16),
        v(share, F32),
    ]
    ag = [dma((2,)), dma((nq - 1,)), dma((1,))]
    rs = [dma((2,)), dma((nz,)), dma((1,))]
    scratch += ag + ag + ag
    scratch += [dma((2,)), dma((nz - 1,)), dma((nz,))]
    scratch += rs + rs
    scratch += [dma((2,)), dma((nq // 2,)), dma((1,))]
    scratch += [dma((4,)), dma((1,)), dma((1,)), dma((1,)), dma((1,))]
    return pl.pallas_call(
        functools.partial(kernel, ny, 1.0 / math.sqrt(nodes)),
        out_shape=(
            jax.ShapeDtypeStruct(block, BF16),
            jax.ShapeDtypeStruct((width, hid), F32),
            jax.ShapeDtypeStruct((hid, width), F32),
        ),
        in_specs=[smem, smem, vmem, vmem, vmem, vmem, vmem],
        out_specs=(vmem, vmem, vmem),
        scratch_shapes=scratch,
        compiler_params=pltpu.CompilerParams(
            collective_id=0, has_side_effects=True, vmem_limit_bytes=48 * 1024 * 1024
        ),
        name="graph_step",
    )(column_ids, block_counts, node_features, adjacency, w1, w2, cotangent)


def build(mesh, ny):
    in_specs = (
        P(("rows", "rep"), None),
        P("rows", "rep", None, None),
        P("rows", "rep"),
        P("rows", "rep"),
        P(),
        P(),
        P(("rows", "rep"), None),
    )
    out_specs = (P(("rows", "rep"), None), P(), P())

    def run(node_features, *rest):
        body = functools.partial(shards, ny, node_features.shape[0])
        return jax.shard_map(
            body, mesh=mesh, in_specs=in_specs, out_specs=out_specs, check_vma=False
        )(node_features, *rest)

    return run


def solution(mesh):
    return build(mesh, NY)
```

time: 650 us -> 99.7 us (0.15)
  waiting for transfers between devices: 562 us -> 0 us
  Pallas kernels: 0 us -> 89.2 us
  matrix products: 34.5 us -> 0 us
  other arithmetic: 20.4 us -> 0 us
  between operations: 14.3 us -> 0.65 us
  local copies, waits for them, and re-layouts: 16.5 us -> 8.87 us
    psum x1 -> x0, waiting for transfers between devices: 241 us -> none  [shards(): lax.psum((local_first, local_second), ('rows', 'rep'))]
    reduce_scatter x3 -> x0, waiting for transfers between devices: 205 us -> none  [the longest x2 144 us: aggregate(): lax.psum_scatter(partial_sum.reshape(row_blocks * BS, feature_width).asty...]
    all_gather x3 -> x0, waiting for transfers between devices: 115 us -> none  [the longest x2 73.8 us: aggregate(): gathered = lax.all_gather(node_field, 'rows', axis=0, tiled=True)]
    pallas_call x0 -> x1, Pallas kernels: none -> 89.2 us  [shards(): pl.pallas_call(functools.partial(kernel, ny, 1.0 / math.sqrt(nodes)), out...]
    dot_general x16 -> x0, matrix products: 34.5 us -> none  [the longest x8 15.9 us: aggregate(): jnp.einsum('rij,rjf->rif', weights, picked, preferred_element_type=jnp.fl...]
    gather x8 -> x0, local copies, waits for them, and re-layouts: 15.5 us -> none  [aggregate(): picked = blocks_in[column_ids[:, slot]]]
    scatter-add x4 -> x0, other arithmetic: 14 us -> none  [transpose_aggregate(): summed = summed.at[column_ids[:, slot]].add(terms)]
    unnamed x26 -> x15, local copies, waits for them, and re-layouts: 0.86 us -> 8.87 us
  transfers between devices with their start and end apart: 7 -> 0, of which waited for: 7 -> 0; matrix products, arithmetic and copies ran while one was open for 11% -> 0% of each run, Pallas kernels for 0% -> 0%
where the time goes in v1:
time: 99.7 us; the launch traced here: 98.7 us
  Pallas kernels  89.2 us (89%)
  local copies, waits for them, and re-layouts  8.87 us (9%)
    pallas_call x1, Pallas kernels, shards(): pl.pallas_call(functools.partial(kernel, ny, 1.0 / math.sqrt(nodes)), out...  89.2 us
    unnamed x15, local copies, waits for them, and re-layouts  8.87 us

profile of v1, /device:TPU:1, one launch (start us, length us, event | category | flops | bytes accessed | tf_op | source)
XLA Modules:
  0.0 98.7 jit_solution(15694998916304382743)
XLA Ops:
  0.6 0.8 copy.10.ids
  1.4 0.7 copy.11.counts
  2.1 0.0 copy-start
  2.1 1.6 %copy-done = bf16[16,4,128,128]{3,2,1,0:T(8,128)(2,1)S(1)} copy-done((bf16[16,4,128,128]{3,2,1,0:T(8,128)(2,1)S(1)}, bf16[16,4,128,128]{3,2,1,0:T(8,128)(2,1)}, u32[]{:S(2)}) %copy-start) | copy-done | bytes 2097176
  3.7 0.0 copy-start.1
  3.7 0.9 copy-done.1
  4.7 0.0 copy-start.2
  4.7 0.9 copy-done.2
  5.6 0.0 copy-start.3
  5.6 0.8 copy-done.3
  6.5 0.0 copy-start.4
  6.5 0.8 copy-done.4
  7.3 89.2 %graph_step.1 = (bf16[128,256]{1,0:T(8,128)(2,1)S(1)}, f32[256,512]{1,0:T(8,128)S(1)}, f32[512,256]{1,0:T(8,128)S(1)}) custom-call(s32[16,4]{1,0:T(8,128)S(1)} %copy.10.ids, s32[16,1]{1,0:T(8,128)S(1)} %copy.11.counts, bf16[128,256]{1,0:T(8,128)(2,1)S(1)} %copy-done.3, bf16[16,4,128,128]{3,2,1,0:T(8,128)(2,1)S(1)} %copy-done, ...), custom_call_target="tpu_custom_call" | custom-call | tf_op jit(solution)/shard_map/graph_step/pallas_call | solution.py:450
  96.5 0.6 copy.15
  97.1 0.8 copy.16
  97.9 0.8 copy.17
Async XLA Ops:
  2.1 1.6 %copy-start = (bf16[16,4,128,128]{3,2,1,0:T(8,128)(2,1)S(1)}, bf16[16,4,128,128]{3,2,1,0:T(8,128)(2,1)}, u32[]{:S(2)}) copy-start(bf16[16,4,128,128]{3,2,1,0:T(8,128)(2,1)} %adj_ref.1) | copy-start | bytes 6291460
  3.7 0.9 copy-start.1
  4.7 0.9 copy-start.2
  5.6 0.8 copy-start.3
  6.5 0.8 copy-start.4

commit v2 on v1

v2 whole, which is shorter than its diff:
```python
import functools
import math

import jax
import jax.numpy as jnp
from jax import lax
from jax.experimental import pallas as pl
from jax.experimental.pallas import tpu as pltpu
from jax.sharding import PartitionSpec as P

MESH = pl.DeviceIdType.MESH
F32 = jnp.float32
BF16 = jnp.bfloat16
VMEM_BYTES = 63 * 1024 * 1024
NL, NX, NY, NZ = 2, 4, 4, 4


def dot(a, b):
    return jnp.dot(a, b, preferred_element_type=F32)


def dot_dims(a, b, ca, cb):
    return lax.dot_general(a, b, (((ca,), (cb,)), ((), ())), preferred_element_type=F32)


def loop(lo, hi, body):
    def step(i, carry):
        body(i)
        return carry

    lax.fori_loop(lo, hi, step, 0)


def kernel(
    scale,
    ids,
    counts,
    x_hbm,
    adj_hbm,
    w1_hbm,
    w2_hbm,
    cot_hbm,
    emb_ref,
    g1_ref,
    g2_ref,
    adj_ref,
    w1_ref,
    w2_ref,
    cot_ref,
    dense,
    feat1,
    feat2,
    cotb,
    terms1,
    terms2,
    hop1,
    hop2,
    ybuf1,
    ybuf2,
    zsend1,
    zsend2,
    zrecv1,
    zrecv2,
    own_sum,
    second,
    tsend,
    trecv,
    town,
    tchip,
    mixed_s,
    hidden_s,
    pre_s,
    glocal,
    gsib,
    gplane,
    gplane_r,
    gline,
    gfin,
    near2,
    near3,
    s_ag1,
    r_ag1,
    f_ag1,
    s_ag2,
    r_ag2,
    f_ag2,
    s_cot,
    rz_cot,
    ry_cot,
    s_rs1,
    rh_rs1,
    ry_rs1,
    rz_rs1,
    s_rs2,
    rh_rs2,
    ry_rs2,
    rz_rs2,
    s_t,
    rs_t,
    rc_t,
    s_g,
    rs_g,
    rp_g,
    rl_g,
    ra_g,
    rf_g,
    s_in,
):
    rows, rep = 2 * NL * NX, NY * NZ
    nq = NL * NX
    bs = x_hbm.shape[0]
    half = bs // 2
    r = lax.axis_index("rows")
    c = lax.axis_index("rep")
    core = lax.rem(r, 2)
    q = r // 2
    l = q // NX
    x = lax.rem(q, NX)
    y = c // NZ
    z = lax.rem(c, NZ)
    sib = (r + 1 - 2 * core, c)

    def xs(d):
        return lax.rem(x + d, NX)

    def ys(d):
        return lax.rem(y + d, NY)

    def zs(d):
        return lax.rem(z + d, NZ)

    def dev(l2=l, x2=x, y2=y, z2=z):
        return ((l2 * NX + x2) * 2 + core, y2 * NZ + z2)

    def chip_at(d):
        return lax.rem(q + d, nq)

    def send(src, dst, ssem, rsem, device):
        pltpu.make_async_remote_copy(
            src_ref=src, dst_ref=dst, send_sem=ssem, recv_sem=rsem, device_id=device, device_id_type=MESH
        ).start()

    def wait(ref, sem):
        pltpu.make_async_copy(ref, ref, sem).wait()

    near = [
        sib,
        dev(l2=1 - l),
        dev(x2=xs(1)),
        dev(x2=xs(2)),
        dev(x2=xs(3)),
        dev(y2=ys(1)),
        dev(y2=ys(3)),
        dev(z2=zs(1)),
        dev(z2=zs(3)),
    ]

    def greet(sem):
        for device in near:
            pl.semaphore_signal(sem, inc=1, device_id=device, device_id_type=MESH)

    def greeted(sem):
        pl.semaphore_wait(sem, len(near))

    barrier = pltpu.get_barrier_semaphore()
    greet(barrier)
    fetch = [
        pltpu.make_async_copy(src, dst, s_in.at[i])
        for i, (src, dst) in enumerate(
            [
                (cot_hbm, cot_ref),
                (x_hbm, feat1.at[core, q]),
                (adj_hbm, adj_ref),
                (w1_hbm, w1_ref),
                (w2_hbm, w2_ref),
            ]
        )
    ]
    for copy in fetch:
        copy.start()

    def gather_start(src, buf, ssem, rsem, fsem):
        to = buf.at[core, q]
        for i, device in enumerate([dev(l2=1 - l), dev(x2=xs(2)), dev(x2=xs(1)), dev(x2=xs(3))]):
            send(src, to, ssem.at[0], rsem.at[i], device)
        send(src, to, ssem.at[0], fsem.at[0], sib)

    def gather_pass(buf, ssem, rsem, fsem, steps):
        there = 1 - l
        came = [
            (there, x, [(4, dev(x2=xs(1))), (5, dev(x2=xs(3)))]),
            (l, xs(2), [(6, dev(l2=there))]),
            (l, xs(3), []),
            (l, xs(1), []),
            (there, xs(3), []),
            (there, xs(1), []),
            (there, xs(2), []),
        ]
        for i in steps:
            l2, x2, onward = came[i]
            block = buf.at[core, l2 * NX + x2]
            wait(block, rsem.at[i])
            for j, device in onward:
                send(block, block, ssem.at[0], rsem.at[j], device)
            send(block, block, ssem.at[1], fsem.at[0], sib)

    def gather_end(buf, fsem):
        wait(buf.at[1 - core], fsem.at[0])

    def gather_sent(buf, ssem):
        wait(buf.at[0], ssem.at[0])
        wait(buf.at[0, pl.ds(0, nq - 1)], ssem.at[1])

    def cot_turn():
        fetch[0].wait()
        cotb[z, y] = cot_ref[...].astype(F32).T.astype(BF16)

    def cot_z(dz):
        own = cotb.at[z, y]
        send(own, own, s_cot.at[0], rz_cot.at[dz - 1], dev(z2=zs(dz)))

    def cot_y(dz):
        block = cotb.at[zs(NZ - dz), y]
        if dz > 0:
            wait(block, rz_cot.at[dz - 1])
        for side, dy in ((0, 1), (1, 3)):
            send(block, block, s_cot.at[1], ry_cot.at[dz, side], dev(y2=ys(dy)))

    def cot_on(dz):
        for side, dy, rows_of in ((0, 1, pl.ds(0, width // 2)), (1, 3, pl.ds(width // 2, width // 2))):
            block = cotb.at[zs(NZ - dz), ys(4 - dy)]
            wait(block, ry_cot.at[dz, side])
            part = block.at[rows_of]
            send(part, part, s_cot.at[1], ry_cot.at[dz, 2], dev(y2=ys(dy)))

    def cot_end():
        for dz in range(NZ):
            wait(cotb.at[zs(NZ - dz), ys(2)], ry_cot.at[dz, 2])

    def cot_sent():
        wait(cotb.at[0, pl.ds(0, NZ - 1)], s_cot.at[0])
        wait(cotb.at[:, pl.ds(0, 3)], s_cot.at[1])

    width = x_hbm.shape[1]

    def densify(b):
        z2 = lax.rem(b, NZ)
        y2 = b // NZ
        blocks = [adj_ref[b, s] for s in range(adj_ref.shape[1])]
        zero = jnp.zeros_like(blocks[0])
        where_to = [jnp.where(s < counts[0, b], ids[s, b], -1) for s in range(len(blocks))]
        row = pl.ds(pl.multiple_of(y2 * bs, bs), bs)
        for p in range(rows):
            total = jnp.where(where_to[0] == p, blocks[0], zero)
            for s in range(1, len(blocks)):
                total = total + jnp.where(where_to[s] == p, blocks[s], zero)
            dense[p % 2, z2, row, (p // 2) * bs : (p // 2 + 1) * bs] = total

    def aggregate_start(feat, terms, hop, ssem, rhsem):
        def one(k):
            z2 = lax.rem(z + k + 1, NZ)
            total = dot(dense[0, z2], feat[0].reshape(nq * bs, -1))
            total = total + dot(dense[1, z2], feat[1].reshape(nq * bs, -1))
            terms[z2] = total.astype(BF16).reshape(terms.shape[1:])
            for side, dy in ((0, 1), (1, 3)):
                part = terms.at[z2, ys(2), pl.ds(side * half, half)]
                send(part, hop.at[k, side], ssem.at[0], rhsem.at[k], dev(y2=ys(dy)))

        loop(0, NZ, one)

    def aggregate_on(k, terms, hop, ybuf, ssem, rhsem, rysem):
        z2 = zs(k + 1)
        wait(hop.at[k], rhsem.at[k])
        for side, dy in ((0, 1), (1, 3)):
            y2 = ys(dy)
            at = pl.ds(side * half, half)
            both = terms[z2, y2, at].astype(F32) + hop[k, side].astype(F32)
            terms[z2, y2, at] = both.astype(BF16)
            send(terms.at[z2, y2], ybuf.at[k, side], ssem.at[0], rysem.at[k], dev(y2=y2))

    def aggregate_fold(k, terms, ybuf, zsend, zrecv, ssem, rysem, rzsem):
        wait(ybuf.at[k], rysem.at[k])
        total = terms[zs(k + 1), y].astype(F32) + ybuf[k, 0].astype(F32) + ybuf[k, 1].astype(F32)
        if k < NZ - 1:
            zsend[k] = total.astype(BF16)
            send(zsend.at[k], zrecv.at[k], ssem.at[1], rzsem.at[0], dev(z2=zs(k + 1)))
        else:
            own_sum[...] = total

    def aggregate_end(zrecv, rzsem):
        wait(zrecv, rzsem.at[0])
        total = own_sum[...]
        for k in range(NZ - 1):
            total = total + zrecv[k].astype(F32)
        return total

    def aggregate_sent(terms, zsend, ssem):
        wait(terms.at[:, pl.ds(0, 3)], ssem.at[0])
        wait(zsend, ssem.at[1])

    def on1(k):
        aggregate_on(k, terms1, hop1, ybuf1, s_rs1, rh_rs1, ry_rs1)

    def on2(k):
        aggregate_on(k, terms2, hop2, ybuf2, s_rs2, rh_rs2, ry_rs2)

    def fold1(k):
        aggregate_fold(k, terms1, ybuf1, zsend1, zrecv1, s_rs1, ry_rs1, rz_rs1)

    def fold2(k):
        aggregate_fold(k, terms2, ybuf2, zsend2, zrecv2, s_rs2, ry_rs2, rz_rs2)

    two = 2 * bs

    def transposed_terms(par, n):
        col = pl.ds(pl.multiple_of(n * two, two), two)
        total = None
        for z2 in range(NZ):
            left = jnp.concatenate([cotb[z2, y2] for y2 in range(NY)], axis=1)
            part = dot(left, dense[par, z2, :, col])
            total = part if total is None else total + part
        return total

    def t_other(n):
        total = transposed_terms(1 - core, n).astype(BF16)
        tsend[2 * n] = total[:, :bs]
        tsend[2 * n + 1] = total[:, bs:]
        pair = pl.ds(2 * n, 2)
        send(tsend.at[pair], trecv.at[pair], s_t.at[0], rs_t.at[n], sib)

    def t_own(n):
        total = transposed_terms(core, n)
        wait(trecv.at[pl.ds(2 * n, 2)], rs_t.at[n])
        town[2 * n] = (total[:, :bs] + trecv[2 * n].astype(F32)).astype(BF16)
        town[2 * n + 1] = (total[:, bs:] + trecv[2 * n + 1].astype(F32)).astype(BF16)

    def t_chips():
        def one(d):
            q2 = chip_at(d)
            send(town.at[q2], tchip.at[d - 1], s_t.at[1], rc_t.at[0], (2 * q2 + core, c))

        loop(1, nq, one)

    def t_sent():
        wait(tsend, s_t.at[0])
        wait(tchip, s_t.at[1])

    def first_layer():
        mixed = aggregate_end(zrecv1, rz_rs1).astype(BF16)
        mixed_s[...] = mixed
        pre = dot(mixed, w1_ref[...])
        pre_s[...] = pre
        hidden = (pre / (1.0 + jnp.exp(-pre))).astype(BF16)
        hidden_s[...] = hidden
        second[...] = dot(hidden, w2_ref[...]).astype(BF16)
        gather_start(second, feat2, s_ag2, r_ag2, f_ag2)
        feat2[core, q] = second[...]

    def gradients():
        wait(tchip, rc_t.at[0])
        up = town[q].astype(F32)
        for d in range(nq - 1):
            up = up + tchip[d].astype(F32)
        up = up.T.astype(BF16)
        second_grad = dot_dims(hidden_s[...], up, 0, 0) * scale
        glocal[1] = jnp.concatenate([second_grad[:width], second_grad[width:]], axis=1).astype(BF16)
        back = dot_dims(up, w2_ref[...], 1, 1)
        pre = pre_s[...]
        gate = 1.0 / (1.0 + jnp.exp(-pre))
        back_pre = (back * gate * (1.0 + pre * (1.0 - gate))).astype(BF16)
        glocal[0] = (dot_dims(mixed_s[...], back_pre, 0, 0) * scale).astype(BF16)
        send(glocal.at[1 - core], gsib, s_g.at[0], rs_g.at[0], sib)

    share = gplane.shape[1]
    place = x * NY + y

    def in_plane(d):
        m = lax.rem(place + d, NX * NY)
        return m, dev(x2=m // NY, y2=lax.rem(m, NY))

    def g_plane():
        wait(gsib, rs_g.at[0])
        both = glocal[core].astype(F32) + gsib[...].astype(F32)
        gplane[...] = both.astype(BF16).reshape(gplane.shape)

        def one(d):
            m, device = in_plane(d)
            send(gplane.at[m], gplane_r.at[d - 1], s_g.at[1], rp_g.at[0], device)

        loop(1, NX * NY, one)

    line = z * NL + l

    def g_line():
        wait(gplane_r, rp_g.at[0])
        total = gplane[place].astype(F32)
        for d in range(NX * NY - 1):
            total = total + gplane_r[d].astype(F32)
        gline[line] = total.astype(BF16)
        own = gline.at[line]

        def one(d):
            there = lax.rem(line + d, NZ * NL)
            send(own, own, s_g.at[2], rl_g.at[0], dev(l2=lax.rem(there, NL), z2=there // NL))

        loop(1, NZ * NL, one)

    def g_gather():
        wait(gline.at[pl.ds(0, NZ * NL - 1)], rl_g.at[0])
        total = gline[0].astype(F32)
        for i in range(1, NZ * NL):
            total = total + gline[i].astype(F32)
        gfin[core, place] = total.astype(BF16)
        own = gfin.at[core, place]
        loop(1, NX * NY, lambda d: send(own, own, s_g.at[3], ra_g.at[0], in_plane(d)[1]))

    def g_core():
        wait(gplane_r, ra_g.at[0])
        send(gfin.at[core], gfin.at[core], s_g.at[4], rf_g.at[0], sib)

    def g_out():
        wait(gfin.at[1 - core], rf_g.at[0])
        g1_ref[...] = gfin[0].reshape(g1_ref.shape).astype(F32)
        second_grad = gfin[1].reshape(g1_ref.shape).astype(F32)
        g2_ref[:width] = second_grad[:, : second_grad.shape[1] // 2]
        g2_ref[width:] = second_grad[:, second_grad.shape[1] // 2 :]

    def g_sent():
        wait(gsib, s_g.at[0])
        wait(gplane_r, s_g.at[1])
        wait(gline.at[pl.ds(0, NZ * NL - 1)], s_g.at[2])
        wait(gplane_r, s_g.at[3])
        wait(gfin.at[0], s_g.at[4])

    cot_turn()
    greeted(barrier)
    greet(near2)
    gather_start(x_hbm, feat1, s_ag1, r_ag1, f_ag1)
    cot_z(1)
    cot_z(3)
    cot_y(0)
    fetch[2].wait()
    loop(0, rep // 2, densify)
    greeted(near2)
    greet(near3)
    cot_z(2)
    gather_pass(feat1, s_ag1, r_ag1, f_ag1, [0])
    cot_y(1)
    cot_y(3)
    gather_pass(feat1, s_ag1, r_ag1, f_ag1, [1])
    loop(rep // 2, rep, densify)
    gather_pass(feat1, s_ag1, r_ag1, f_ag1, range(2, 7))
    cot_y(2)
    cot_on(0)
    fetch[1].wait()
    gather_end(feat1, f_ag1)
    aggregate_start(feat1, terms1, hop1, s_rs1, rh_rs1)
    cot_on(1)
    cot_on(3)
    loop(0, NZ, on1)
    cot_on(2)
    cot_end()
    loop(0, nq // 2, t_other)
    fold1(0)
    loop(0, nq // 2, t_own)
    fold1(1)
    t_chips()
    fold1(2)
    fold1(3)
    greeted(near3)
    fetch[3].wait()
    fetch[4].wait()
    first_layer()
    gradients()
    gather_pass(feat2, s_ag2, r_ag2, f_ag2, [0, 1])
    g_plane()
    gather_pass(feat2, s_ag2, r_ag2, f_ag2, range(2, 7))
    gather_end(feat2, f_ag2)
    aggregate_start(feat2, terms2, hop2, s_rs2, rh_rs2)
    g_line()
    loop(0, NZ, on2)
    fold2(0)
    g_gather()
    fold2(1)
    fold2(2)
    fold2(3)
    g_core()
    emb_ref[...] = aggregate_end(zrecv2, rz_rs2).astype(BF16)
    g_out()

    gather_sent(feat1, s_ag1)
    cot_sent()
    aggregate_sent(terms1, zsend1, s_rs1)
    gather_sent(feat2, s_ag2)
    aggregate_sent(terms2, zsend2, s_rs2)
    t_sent()
    g_sent()


def shards(nodes, node_features, adjacency, column_ids, block_counts, w1, w2, cotangent):
    rep, nq = NY * NZ, NL * NX
    bs, width = node_features.shape
    hid = w1.shape[1]
    block = (bs, width)
    turned = (width, bs)
    share = (width // (NX * NY), hid)
    vmem = pl.BlockSpec(memory_space=pltpu.VMEM)
    smem = pl.BlockSpec(memory_space=pltpu.SMEM)
    hbm = pl.BlockSpec(memory_space=pl.ANY)
    v = pltpu.VMEM
    dma = pltpu.SemaphoreType.DMA
    scratch = [
        v(adjacency.shape, BF16),
        v(w1.shape, BF16),
        v(w2.shape, BF16),
        v(block, BF16),
        v((2, NZ, NY * bs, nq * bs), BF16),
        v((2, nq) + block, BF16),
        v((2, nq) + block, BF16),
        v((NZ, NY) + turned, BF16),
        v((NZ, NY) + block, BF16),
        v((NZ, NY) + block, BF16),
        v((NZ, 2, bs // 2, width), BF16),
        v((NZ, 2, bs // 2, width), BF16),
        v((NZ, 2) + block, BF16),
        v((NZ, 2) + block, BF16),
        v((NZ - 1,) + block, BF16),
        v((NZ - 1,) + block, BF16),
        v((NZ - 1,) + block, BF16),
        v((NZ - 1,) + block, BF16),
        v(block, F32),
        v(block, BF16),
        v((nq,) + turned, BF16),
        v((nq,) + turned, BF16),
        v((nq,) + turned, BF16),
        v((nq - 1,) + turned, BF16),
        v(block, BF16),
        v((bs, hid), BF16),
        v((bs, hid), F32),
        v((2, width, hid), BF16),
        v((width, hid), BF16),
        v((NX * NY,) + share, BF16),
        v((NX * NY - 1,) + share, BF16),
        v((NZ * NL,) + share, BF16),
        v((2, NX * NY) + share, BF16),
        pltpu.SemaphoreType.REGULAR,
        pltpu.SemaphoreType.REGULAR,
    ]
    ag = [dma((2,)), dma((7,)), dma((1,))]
    rs = [dma((2,)), dma((NZ,)), dma((NZ,)), dma((1,))]
    scratch += ag + ag
    scratch += [dma((2,)), dma((NZ - 1,)), dma((NZ, 3))]
    scratch += rs + rs
    scratch += [dma((2,)), dma((nq // 2,)), dma((1,))]
    scratch += [dma((5,)), dma((1,)), dma((1,)), dma((1,)), dma((1,)), dma((1,)), dma((5,))]
    return pl.pallas_call(
        functools.partial(kernel, 1.0 / math.sqrt(nodes)),
        out_shape=(
            jax.ShapeDtypeStruct(block, BF16),
            jax.ShapeDtypeStruct((width, hid), F32),
            jax.ShapeDtypeStruct((hid, width), F32),
        ),
        in_specs=[smem, smem, hbm, hbm, hbm, hbm, hbm],
        out_specs=(vmem, vmem, vmem),
        scratch_shapes=scratch,
        compiler_params=pltpu.CompilerParams(
            collective_id=0, has_side_effects=True, vmem_limit_bytes=VMEM_BYTES
        ),
        name="graph_step",
    )(column_ids.T, block_counts.T, node_features, adjacency, w1, w2, cotangent)


def solution(mesh):
    in_specs = (
        P(("rows", "rep"), None),
        P("rows", "rep", None, None),
        P("rows", "rep"),
        P("rows", "rep"),
        P(),
        P(),
        P(("rows", "rep"), None),
    )
    out_specs = (P(("rows", "rep"), None), P(), P())

    def run(node_features, *rest):
        body = functools.partial(shards, node_features.shape[0])
        return jax.shard_map(
            body, mesh=mesh, in_specs=in_specs, out_specs=out_specs, check_vma=False
        )(node_features, *rest)

    return run
```

time: 99.7 us -> 89.3 us (0.90)
  Pallas kernels: 89.2 us -> 83.1 us
  local copies, waits for them, and re-layouts: 8.87 us -> 5.21 us
    pallas_call x1, Pallas kernels: 89.2 us -> 83.1 us  [shards(): pl.pallas_call(functools.partial(kernel, 1.0 / math.sqrt(nodes)), out_sha...]
    unnamed x15 -> x3, local copies, waits for them, and re-layouts: 8.87 us -> 5.21 us
where the time goes in v2:
time: 89.3 us; the launch traced here: 89 us
  Pallas kernels  83.1 us (93%)
  local copies, waits for them, and re-layouts  5.21 us (6%)
    pallas_call x1, Pallas kernels, shards(): pl.pallas_call(functools.partial(kernel, 1.0 / math.sqrt(nodes)), out_sha...  83.1 us
    unnamed x3, local copies, waits for them, and re-layouts  5.21 us

profile of v2, /device:TPU:1, one launch (start us, length us, event | category | flops | bytes accessed | tf_op | source)
XLA Modules:
  0.0 89.0 jit_solution(9318929867507083368)
XLA Ops:
  0.6 83.1 %graph_step.1 = (bf16[128,256]{1,0:T(8,128)(2,1)}, f32[256,512]{1,0:T(8,128)}, f32[512,256]{1,0:T(8,128)}) custom-call(s32[4,16]{1,0:T(4,128)} %bitcast.2, s32[1,16]{1,0:T(1,128)} %bitcast.3, bf16[128,256]{1,0:T(8,128)(2,1)} %x_hbm.1, bf16[16,4,128,128]{3,2,1,0:T(8,128)(2,1)} %adj_hbm.1, bf16[256,512]{1,0:T(8,128)(2,1)} %w1_hbm.1, bf16[512,256]{1,0:T(8,128)(2,1)} %w2_hbm.1, ...), custom_call_target="tpu_custom_call" | custom-call | tf_op jit(solution)/shard_map/graph_step/pallas_call | solution.py:556
  83.8 1.5 %copy.13 = bf16[128,256]{1,0:T(8,128)(2,1)} copy(bf16[128,256]{1,0:T(8,128)(2,1)} %get-tuple-element.6) | data formatting | bytes 131072
  85.3 1.9 %copy.14 = f32[256,512]{1,0:T(8,128)} copy(f32[256,512]{1,0:T(8,128)} %get-tuple-element.7) | data formatting | bytes 1048576
  87.1 1.9 %copy.15 = f32[512,256]{1,0:T(8,128)} copy(f32[512,256]{1,0:T(8,128)} %get-tuple-element.8) | data formatting | bytes 1048576

commit v3 on v2

--- a/solution.py
+++ b/solution.py
@@ -13,6 +13,7 @@
 BF16 = jnp.bfloat16
 VMEM_BYTES = 63 * 1024 * 1024
 NL, NX, NY, NZ = 2, 4, 4, 4
+AHEAD = 2
 
 
 def dot(a, b):
@@ -40,9 +41,8 @@
     w1_hbm,
     w2_hbm,
     cot_hbm,
-    emb_ref,
-    g1_ref,
-    g2_ref,
+    emb_hbm,
+    g_hbm,
     adj_ref,
     w1_ref,
     w2_ref,
@@ -63,6 +63,7 @@
     zrecv2,
     own_sum,
     second,
+    emb_s,
     tsend,
     trecv,
     town,
@@ -105,6 +106,7 @@
     ra_g,
     rf_g,
     s_in,
+    s_out,
 ):
     rows, rep = 2 * NL * NX, NY * NZ
     nq = NL * NX
@@ -164,6 +166,9 @@
 
     barrier = pltpu.get_barrier_semaphore()
     greet(barrier)
+    emb_out = pltpu.make_async_copy(emb_s, emb_hbm, s_out.at[0])
+    g_own_out = pltpu.make_async_copy(gfin.at[core], g_hbm.at[core], s_out.at[1])
+    g_sib_out = pltpu.make_async_copy(gfin.at[1 - core], g_hbm.at[1 - core], s_out.at[2])
     fetch = [
         pltpu.make_async_copy(src, dst, s_in.at[i])
         for i, (src, dst) in enumerate(
@@ -249,41 +254,49 @@
         blocks = [adj_ref[b, s] for s in range(adj_ref.shape[1])]
         zero = jnp.zeros_like(blocks[0])
         where_to = [jnp.where(s < counts[0, b], ids[s, b], -1) for s in range(len(blocks))]
-        row = pl.ds(pl.multiple_of(y2 * bs, bs), bs)
+        row = pl.ds(pl.multiple_of(z2 * bs, bs), bs)
         for p in range(rows):
             total = jnp.where(where_to[0] == p, blocks[0], zero)
             for s in range(1, len(blocks)):
                 total = total + jnp.where(where_to[s] == p, blocks[s], zero)
-            dense[p % 2, z2, row, (p // 2) * bs : (p // 2 + 1) * bs] = total
+            dense[p % 2, y2, row, (p // 2) * bs : (p // 2 + 1) * bs] = total
+
+    sides = ((0, 1), (1, 3))
+    dz_order = (2, 1, 3, 0)
 
     def aggregate_start(feat, terms, hop, ssem, rhsem):
-        def one(k):
-            z2 = lax.rem(z + k + 1, NZ)
-            total = dot(dense[0, z2], feat[0].reshape(nq * bs, -1))
-            total = total + dot(dense[1, z2], feat[1].reshape(nq * bs, -1))
-            terms[z2] = total.astype(BF16).reshape(terms.shape[1:])
-            for side, dy in ((0, 1), (1, 3)):
-                part = terms.at[z2, ys(2), pl.ds(side * half, half)]
-                send(part, hop.at[k, side], ssem.at[0], rhsem.at[k], dev(y2=ys(dy)))
-
-        loop(0, NZ, one)
+        def one(dy):
+            y2 = lax.rem(y + dy, NY)
+            total = dot(dense[0, y2], feat[0].reshape(nq * bs, -1))
+            total = total + dot(dense[1, y2], feat[1].reshape(nq * bs, -1))
+            terms[y2] = total.astype(BF16).reshape(terms.shape[1:])
+
+        one(2)
+        for k, dz in enumerate(dz_order):
+            for side, dy in sides:
+                part = terms.at[ys(2), zs(dz), pl.ds(side * half, half)]
+                send(part, hop.at[k, side], ssem.at[NZ], rhsem.at[k], dev(y2=ys(dy)))
+        loop(0, 3, lambda i: one(1 + 2 * i - i // 2))
 
     def aggregate_on(k, terms, hop, ybuf, ssem, rhsem, rysem):
-        z2 = zs(k + 1)
+        z2 = zs(dz_order[k])
         wait(hop.at[k], rhsem.at[k])
-        for side, dy in ((0, 1), (1, 3)):
+        if k >= AHEAD:
+            wait(ybuf.at[k - AHEAD], ssem.at[k - AHEAD])
+        for side, dy in sides:
             y2 = ys(dy)
             at = pl.ds(side * half, half)
-            both = terms[z2, y2, at].astype(F32) + hop[k, side].astype(F32)
-            terms[z2, y2, at] = both.astype(BF16)
-            send(terms.at[z2, y2], ybuf.at[k, side], ssem.at[0], rysem.at[k], dev(y2=y2))
+            both = terms[y2, z2, at].astype(F32) + hop[k, side].astype(F32)
+            terms[y2, z2, at] = both.astype(BF16)
+            send(terms.at[y2, z2], ybuf.at[k, side], ssem.at[k], rysem.at[k], dev(y2=y2))
 
     def aggregate_fold(k, terms, ybuf, zsend, zrecv, ssem, rysem, rzsem):
+        dz = dz_order[k]
         wait(ybuf.at[k], rysem.at[k])
-        total = terms[zs(k + 1), y].astype(F32) + ybuf[k, 0].astype(F32) + ybuf[k, 1].astype(F32)
-        if k < NZ - 1:
+        total = terms[y, zs(dz)].astype(F32) + ybuf[k, 0].astype(F32) + ybuf[k, 1].astype(F32)
+        if dz:
             zsend[k] = total.astype(BF16)
-            send(zsend.at[k], zrecv.at[k], ssem.at[1], rzsem.at[0], dev(z2=zs(k + 1)))
+            send(zsend.at[k], zrecv.at[k], ssem.at[NZ + 1], rzsem.at[0], dev(z2=zs(dz)))
         else:
             own_sum[...] = total
 
@@ -292,11 +305,13 @@
         total = own_sum[...]
         for k in range(NZ - 1):
             total = total + zrecv[k].astype(F32)
-        return total
-
-    def aggregate_sent(terms, zsend, ssem):
-        wait(terms.at[:, pl.ds(0, 3)], ssem.at[0])
-        wait(zsend, ssem.at[1])
+        return total.astype(BF16)
+
+    def aggregate_sent(hop, ybuf, zsend, ssem):
+        wait(hop, ssem.at[NZ])
+        wait(zsend, ssem.at[NZ + 1])
+        for k in range(NZ - AHEAD, NZ):
+            wait(ybuf.at[k], ssem.at[k])
 
     def on1(k):
         aggregate_on(k, terms1, hop1, ybuf1, s_rs1, rh_rs1, ry_rs1)
@@ -315,9 +330,9 @@
     def transposed_terms(par, n):
         col = pl.ds(pl.multiple_of(n * two, two), two)
         total = None
-        for z2 in range(NZ):
-            left = jnp.concatenate([cotb[z2, y2] for y2 in range(NY)], axis=1)
-            part = dot(left, dense[par, z2, :, col])
+        for y2 in range(NY):
+            left = jnp.concatenate([cotb[z2, y2] for z2 in range(NZ)], axis=1)
+            part = dot(left, dense[par, y2, :, col])
             total = part if total is None else total + part
         return total
 
@@ -346,7 +361,7 @@
         wait(tchip, s_t.at[1])
 
     def first_layer():
-        mixed = aggregate_end(zrecv1, rz_rs1).astype(BF16)
+        mixed = aggregate_end(zrecv1, rz_rs1)
         mixed_s[...] = mixed
         pre = dot(mixed, w1_ref[...])
         pre_s[...] = pre
@@ -417,13 +432,13 @@
     def g_core():
         wait(gplane_r, ra_g.at[0])
         send(gfin.at[core], gfin.at[core], s_g.at[4], rf_g.at[0], sib)
+        g_own_out.start()
 
     def g_out():
         wait(gfin.at[1 - core], rf_g.at[0])
-        g1_ref[...] = gfin[0].reshape(g1_ref.shape).astype(F32)
-        second_grad = gfin[1].reshape(g1_ref.shape).astype(F32)
-        g2_ref[:width] = second_grad[:, : second_grad.shape[1] // 2]
-        g2_ref[width:] = second_grad[:, second_grad.shape[1] // 2 :]
+        g_sib_out.start()
+        g_own_out.wait()
+        g_sib_out.wait()
 
     def g_sent():
         wait(gsib, s_g.at[0])
@@ -450,23 +465,26 @@
     gather_pass(feat1, s_ag1, r_ag1, f_ag1, [1])
     loop(rep // 2, rep, densify)
     gather_pass(feat1, s_ag1, r_ag1, f_ag1, range(2, 7))
+    cot_on(0)
     cot_y(2)
-    cot_on(0)
     fetch[1].wait()
     gather_end(feat1, f_ag1)
     aggregate_start(feat1, terms1, hop1, s_rs1, rh_rs1)
     cot_on(1)
     cot_on(3)
-    loop(0, NZ, on1)
+    on1(0)
+    on1(1)
+    on1(2)
+    on1(3)
     cot_on(2)
+    fold1(0)
+    fold1(1)
+    fold1(2)
+    fold1(3)
     cot_end()
     loop(0, nq // 2, t_other)
-    fold1(0)
     loop(0, nq // 2, t_own)
-    fold1(1)
     t_chips()
-    fold1(2)
-    fold1(3)
     greeted(near3)
     fetch[3].wait()
     fetch[4].wait()
@@ -474,27 +492,55 @@
     gradients()
     gather_pass(feat2, s_ag2, r_ag2, f_ag2, [0, 1])
     g_plane()
-    gather_pass(feat2, s_ag2, r_ag2, f_ag2, range(2, 7))
+    gather_pass(feat2, s_ag2, r_ag2, f_ag2, [2, 3, 4, 5, 6])
     gather_end(feat2, f_ag2)
     aggregate_start(feat2, terms2, hop2, s_rs2, rh_rs2)
     g_line()
-    loop(0, NZ, on2)
+    on2(0)
+    on2(1)
+    on2(2)
+    on2(3)
     fold2(0)
     g_gather()
     fold2(1)
     fold2(2)
     fold2(3)
     g_core()
-    emb_ref[...] = aggregate_end(zrecv2, rz_rs2).astype(BF16)
+    emb_s[...] = aggregate_end(zrecv2, rz_rs2)
+    emb_out.start()
     g_out()
+    emb_out.wait()
 
     gather_sent(feat1, s_ag1)
     cot_sent()
-    aggregate_sent(terms1, zsend1, s_rs1)
+    aggregate_sent(hop1, ybuf1, zsend1, s_rs1)
     gather_sent(feat2, s_ag2)
-    aggregate_sent(terms2, zsend2, s_rs2)
+    aggregate_sent(hop2, ybuf2, zsend2, s_rs2)
     t_sent()
     g_sent()
+
+
+def finish(emb_in, g_in, emb_out, g1_out, g2_out, g_s, g1_s, g2_s, sems):
+    width = g1_s.shape[0]
+    emb = pltpu.make_async_copy(emb_in, emb_out, sems.at[0])
+    first_in = pltpu.make_async_copy(g_in.at[0], g_s.at[0], sems.at[1])
+    second_in = pltpu.make_async_copy(g_in.at[1], g_s.at[1], sems.at[2])
+    first_out = pltpu.make_async_copy(g1_s, g1_out, sems.at[3])
+    second_out = pltpu.make_async_copy(g2_s, g2_out, sems.at[4])
+    first_in.start()
+    second_in.start()
+    emb.start()
+    first_in.wait()
+    g1_s[...] = g_s[0].reshape(g1_s.shape).astype(F32)
+    first_out.start()
+    second_in.wait()
+    grad = g_s[1].reshape(g1_s.shape).astype(F32)
+    g2_s[:width] = grad[:, :width]
+    g2_s[width:] = grad[:, width:]
+    second_out.start()
+    emb.wait()
+    first_out.wait()
+    second_out.wait()
 
 
 def shards(nodes, node_features, adjacency, column_ids, block_counts, w1, w2, cotangent):
@@ -514,12 +560,12 @@
         v(w1.shape, BF16),
         v(w2.shape, BF16),
         v(block, BF16),
-        v((2, NZ, NY * bs, nq * bs), BF16),
+        v((2, NY, NZ * bs, nq * bs), BF16),
         v((2, nq) + block, BF16),
         v((2, nq) + block, BF16),
         v((NZ, NY) + turned, BF16),
-        v((NZ, NY) + block, BF16),
-        v((NZ, NY) + block, BF16),
+        v((NY, NZ) + block, BF16),
+        v((NY, NZ) + block, BF16),
         v((NZ, 2, bs // 2, width), BF16),
         v((NZ, 2, bs // 2, width), BF16),
         v((NZ, 2) + block, BF16),
@@ -529,6 +575,7 @@
         v((NZ - 1,) + block, BF16),
         v((NZ - 1,) + block, BF16),
         v(block, F32),
+        v(block, BF16),
         v(block, BF16),
         v((nq,) + turned, BF16),
         v((nq,) + turned, BF16),
@@ -547,27 +594,44 @@
         pltpu.SemaphoreType.REGULAR,
     ]
     ag = [dma((2,)), dma((7,)), dma((1,))]
-    rs = [dma((2,)), dma((NZ,)), dma((NZ,)), dma((1,))]
+    rs = [dma((NZ + 2,)), dma((NZ,)), dma((NZ,)), dma((1,))]
     scratch += ag + ag
     scratch += [dma((2,)), dma((NZ - 1,)), dma((NZ, 3))]
     scratch += rs + rs
     scratch += [dma((2,)), dma((nq // 2,)), dma((1,))]
-    scratch += [dma((5,)), dma((1,)), dma((1,)), dma((1,)), dma((1,)), dma((1,)), dma((5,))]
-    return pl.pallas_call(
+    scratch += [dma((5,)), dma((1,)), dma((1,)), dma((1,)), dma((1,)), dma((1,)), dma((5,)), dma((3,))]
+    embedding, grads = pl.pallas_call(
         functools.partial(kernel, 1.0 / math.sqrt(nodes)),
         out_shape=(
             jax.ShapeDtypeStruct(block, BF16),
-            jax.ShapeDtypeStruct((width, hid), F32),
-            jax.ShapeDtypeStruct((hid, width), F32),
+            jax.ShapeDtypeStruct((2, NX * NY) + share, BF16),
         ),
         in_specs=[smem, smem, hbm, hbm, hbm, hbm, hbm],
-        out_specs=(vmem, vmem, vmem),
+        out_specs=(hbm, hbm),
         scratch_shapes=scratch,
         compiler_params=pltpu.CompilerParams(
             collective_id=0, has_side_effects=True, vmem_limit_bytes=VMEM_BYTES
         ),
         name="graph_step",
     )(column_ids.T, block_counts.T, node_features, adjacency, w1, w2, cotangent)
+    return pl.pallas_call(
+        finish,
+        out_shape=(
+            jax.ShapeDtypeStruct(block, BF16),
+            jax.ShapeDtypeStruct((width, hid), F32),
+            jax.ShapeDtypeStruct((hid, width), F32),
+        ),
+        in_specs=[hbm, hbm],
+        out_specs=(hbm, hbm, hbm),
+        scratch_shapes=[
+            v(grads.shape, BF16),
+            v((width, hid), F32),
+            v((hid, width), F32),
+            dma((5,)),
+        ],
+        compiler_params=pltpu.CompilerParams(vmem_limit_bytes=VMEM_BYTES),
+        name="finish",
+    )(embedding, grads)
 
 
 def solution(mesh):

time: 89.3 us -> 79.1 us (0.89)
  local copies, waits for them, and re-layouts: 5.21 us -> 0 us
  Pallas kernels: 83.1 us -> 78.3 us
    pallas_call x1, Pallas kernels: 83.1 us -> 75.2 us  [shards(): pl.pallas_call(functools.partial(kernel, 1.0 / math.sqrt(nodes)), out_sha...]
    unnamed x3 -> x0, local copies, waits for them, and re-layouts: 5.21 us -> none
    pallas_call x0 -> x1, Pallas kernels: none -> 3.14 us  [shards(): pl.pallas_call(finish, out_shape=(jax.ShapeDtypeStruct(block, BF16), jax....]
where the time goes in v3:
time: 79.1 us; the launch traced here: 78.9 us
  Pallas kernels  78.3 us (99%)
    pallas_call x1, Pallas kernels, shards(): pl.pallas_call(functools.partial(kernel, 1.0 / math.sqrt(nodes)), out_sha...  75.2 us
    pallas_call x1, Pallas kernels, shards(): pl.pallas_call(finish, out_shape=(jax.ShapeDtypeStruct(block, BF16), jax....  3.14 us

profile of v3, /device:TPU:1, one launch (start us, length us, event | category | flops | bytes accessed | tf_op | source)
XLA Modules:
  0.0 78.9 jit_solution(9017701578732234724)
XLA Ops:
  0.6 75.2 %graph_step.1 = (bf16[128,256]{1,0:T(8,128)(2,1)}, bf16[2,16,16,512]{3,2,1,0:T(8,128)(2,1)}) custom-call(s32[4,16]{1,0:T(4,128)} %bitcast.2, s32[1,16]{1,0:T(1,128)} %bitcast.3, bf16[128,256]{1,0:T(8,128)(2,1)} %x_hbm.1, bf16[16,4,128,128]{3,2,1,0:T(8,128)(2,1)} %adj_hbm.1, bf16[256,512]{1,0:T(8,128)(2,1)} %w1_hbm.1, bf16[512,256]{1,0:T(8,128)(2,1)} %w2_hbm.1, ...), custom_call_target="tpu_custom_call" | custom-call | tf_op jit(solution)/shard_map/graph_step/pallas_call | solution.py:603
  75.8 3.1 %finish.1 = (bf16[128,256]{1,0:T(8,128)(2,1)}, f32[256,512]{1,0:T(8,128)}, f32[512,256]{1,0:T(8,128)}) custom-call(bf16[128,256]{1,0:T(8,128)(2,1)} %get-tuple-element.5.emb_in, bf16[2,16,16,512]{3,2,1,0:T(8,128)(2,1)} %get-tuple-element.6.g_in), custom_call_target="tpu_custom_call" | custom-call | tf_op jit(solution)/shard_map/finish/pallas_call | solution.py:617

commit v4 on v3

--- a/solution.py
+++ b/solution.py
@@ -13,7 +13,8 @@
 BF16 = jnp.bfloat16
 VMEM_BYTES = 63 * 1024 * 1024
 NL, NX, NY, NZ = 2, 4, 4, 4
-AHEAD = 2
+AHEAD = 4
+TAIL = 16
 
 
 def dot(a, b):
@@ -54,7 +55,9 @@
     terms1,
     terms2,
     hop1,
-    hop2,
+    zfirst,
+    ztail,
+    ytail,
     ybuf1,
     ybuf2,
     zsend1,
@@ -64,6 +67,7 @@
     own_sum,
     second,
     emb_s,
+    tnear,
     tsend,
     trecv,
     town,
@@ -93,9 +97,9 @@
     ry_rs1,
     rz_rs1,
     s_rs2,
-    rh_rs2,
     ry_rs2,
     rz_rs2,
+    rf_rs2,
     s_t,
     rs_t,
     rc_t,
@@ -316,35 +320,91 @@
     def on1(k):
         aggregate_on(k, terms1, hop1, ybuf1, s_rs1, rh_rs1, ry_rs1)
 
-    def on2(k):
-        aggregate_on(k, terms2, hop2, ybuf2, s_rs2, rh_rs2, ry_rs2)
-
     def fold1(k):
         aggregate_fold(k, terms1, ybuf1, zsend1, zrecv1, s_rs1, ry_rs1, rz_rs1)
 
-    def fold2(k):
-        aggregate_fold(k, terms2, ybuf2, zsend2, zrecv2, s_rs2, ry_rs2, rz_rs2)
+    upper = bs - TAIL
+
+    def second_start():
+        def one(k, dz, away):
+            z2 = zs(dz)
+            row = pl.ds(pl.multiple_of(z2 * bs, bs), bs)
+            total = None
+            for par in range(2):
+                left = jnp.concatenate([dense[par, y2, row] for y2 in range(NY)], axis=0)
+                part = dot(left, feat2[par].reshape(nq * bs, -1))
+                total = part if total is None else total + part
+            terms2[z2] = total.astype(BF16).reshape(terms2.shape[1:])
+            if away:
+                part = terms2.at[z2, :, pl.ds(upper, TAIL)]
+                send(part, zfirst.at[dz - 1], s_rs2.at[2], rf_rs2.at[0], dev(z2=z2))
+            for i, dy in enumerate((2, 1, 3)):
+                part = terms2.at[z2, ys(dy), pl.ds(0, upper)]
+                send(part, ybuf2.at[k, i], s_rs2.at[0], ry_rs2.at[k], dev(y2=ys(dy)))
+
+        loop(0, NZ - 1, lambda k: one(k, 2 - k + 3 * (k // 2), True))
+        one(NZ - 1, 0, False)
+
+    def second_tail():
+        wait(zfirst, rf_rs2.at[0])
+        total = terms2[z, :, upper:].astype(F32)
+        for i in range(NZ - 1):
+            total = total + zfirst[i].astype(F32)
+        ztail[...] = total.astype(BF16)
+        for i, dy in enumerate((2, 1, 3)):
+            send(ztail.at[ys(dy)], ytail.at[i], s_rs2.at[3], rf_rs2.at[1], dev(y2=ys(dy)))
+
+    def second_fold(k):
+        dz = dz_order[k]
+        wait(ybuf2.at[k], ry_rs2.at[k])
+        total = terms2[zs(dz), y, :upper].astype(F32)
+        for i in range(NY - 1):
+            total = total + ybuf2[k, i].astype(F32)
+        if dz:
+            zsend2[k] = total.astype(BF16)
+            send(zsend2.at[k], zrecv2.at[k], s_rs2.at[1], rz_rs2.at[0], dev(z2=zs(dz)))
+        else:
+            own_sum[:upper] = total
+
+    def second_end():
+        wait(ytail, rf_rs2.at[1])
+        low = ztail[y].astype(F32)
+        for i in range(NY - 1):
+            low = low + ytail[i].astype(F32)
+        wait(zrecv2, rz_rs2.at[0])
+        total = own_sum[:upper]
+        for k in range(NZ - 1):
+            total = total + zrecv2[k].astype(F32)
+        emb_s[:upper] = total.astype(BF16)
+        emb_s[upper:] = low.astype(BF16)
+
+    def second_sent():
+        wait(ybuf2, s_rs2.at[0])
+        wait(zsend2, s_rs2.at[1])
+        wait(zfirst, s_rs2.at[2])
+        wait(ytail, s_rs2.at[3])
 
     two = 2 * bs
 
-    def transposed_terms(par, n):
+    def transposed_part(par, n, y2):
         col = pl.ds(pl.multiple_of(n * two, two), two)
-        total = None
-        for y2 in range(NY):
-            left = jnp.concatenate([cotb[z2, y2] for z2 in range(NZ)], axis=1)
-            part = dot(left, dense[par, y2, :, col])
-            total = part if total is None else total + part
-        return total
+        left = jnp.concatenate([cotb[z2, y2] for z2 in range(NZ)], axis=1)
+        return dot(left, dense[par, y2, :, col])
+
+    def t_near(i):
+        par, n = i // (nq // 2), lax.rem(i, nq // 2)
+        total = transposed_part(par, n, y) + transposed_part(par, n, ys(1))
+        tnear[par, n] = total + transposed_part(par, n, ys(3))
 
     def t_other(n):
-        total = transposed_terms(1 - core, n).astype(BF16)
+        total = (tnear[1 - core, n] + transposed_part(1 - core, n, ys(2))).astype(BF16)
         tsend[2 * n] = total[:, :bs]
         tsend[2 * n + 1] = total[:, bs:]
         pair = pl.ds(2 * n, 2)
         send(tsend.at[pair], trecv.at[pair], s_t.at[0], rs_t.at[n], sib)
 
     def t_own(n):
-        total = transposed_terms(core, n)
+        total = tnear[core, n] + transposed_part(core, n, ys(2))
         wait(trecv.at[pl.ds(2 * n, 2)], rs_t.at[n])
         town[2 * n] = (total[:, :bs] + trecv[2 * n].astype(F32)).astype(BF16)
         town[2 * n + 1] = (total[:, bs:] + trecv[2 * n + 1].astype(F32)).astype(BF16)
@@ -477,36 +537,35 @@
     on1(2)
     on1(3)
     cot_on(2)
+    loop(0, nq, t_near)
     fold1(0)
     fold1(1)
-    fold1(2)
-    fold1(3)
     cot_end()
     loop(0, nq // 2, t_other)
+    fold1(2)
     loop(0, nq // 2, t_own)
     t_chips()
+    fold1(3)
     greeted(near3)
     fetch[3].wait()
     fetch[4].wait()
     first_layer()
+    gather_pass(feat2, s_ag2, r_ag2, f_ag2, [0])
     gradients()
-    gather_pass(feat2, s_ag2, r_ag2, f_ag2, [0, 1])
+    gather_pass(feat2, s_ag2, r_ag2, f_ag2, [1])
     g_plane()
     gather_pass(feat2, s_ag2, r_ag2, f_ag2, [2, 3, 4, 5, 6])
     gather_end(feat2, f_ag2)
-    aggregate_start(feat2, terms2, hop2, s_rs2, rh_rs2)
+    second_start()
     g_line()
-    on2(0)
-    on2(1)
-    on2(2)
-    on2(3)
-    fold2(0)
+    second_fold(0)
+    second_fold(1)
+    second_tail()
     g_gather()
-    fold2(1)
-    fold2(2)
-    fold2(3)
+    second_fold(2)
+    second_fold(3)
     g_core()
-    emb_s[...] = aggregate_end(zrecv2, rz_rs2)
+    second_end()
     emb_out.start()
     g_out()
     emb_out.wait()
@@ -515,7 +574,7 @@
     cot_sent()
     aggregate_sent(hop1, ybuf1, zsend1, s_rs1)
     gather_sent(feat2, s_ag2)
-    aggregate_sent(hop2, ybuf2, zsend2, s_rs2)
+    second_sent()
     t_sent()
     g_sent()
 
@@ -549,6 +608,7 @@
     hid = w1.shape[1]
     block = (bs, width)
     turned = (width, bs)
+    upper = (bs - TAIL, width)
     share = (width // (NX * NY), hid)
     vmem = pl.BlockSpec(memory_space=pltpu.VMEM)
     smem = pl.BlockSpec(memory_space=pltpu.SMEM)
@@ -567,16 +627,19 @@
         v((NY, NZ) + block, BF16),
         v((NY, NZ) + block, BF16),
         v((NZ, 2, bs // 2, width), BF16),
-        v((NZ, 2, bs // 2, width), BF16),
+        v((NZ - 1, NY, TAIL, width), BF16),
+        v((NY, TAIL, width), BF16),
+        v((NY - 1, TAIL, width), BF16),
         v((NZ, 2) + block, BF16),
-        v((NZ, 2) + block, BF16),
+        v((NZ, NY - 1) + upper, BF16),
         v((NZ - 1,) + block, BF16),
+        v((NZ - 1,) + upper, BF16),
         v((NZ - 1,) + block, BF16),
-        v((NZ - 1,) + block, BF16),
-        v((NZ - 1,) + block, BF16),
+        v((NZ - 1,) + upper, BF16),
         v(block, F32),
         v(block, BF16),
         v(block, BF16),
+        v((2, nq // 2, width, 2 * bs), F32),
         v((nq,) + turned, BF16),
         v((nq,) + turned, BF16),
         v((nq,) + turned, BF16),
@@ -597,7 +660,7 @@
     rs = [dma((NZ + 2,)), dma((NZ,)), dma((NZ,)), dma((1,))]
     scratch += ag + ag
     scratch += [dma((2,)), dma((NZ - 1,)), dma((NZ, 3))]
-    scratch += rs + rs
+    scratch += rs + [dma((4,)), dma((NZ,)), dma((1,)), dma((2,))]
     scratch += [dma((2,)), dma((nq // 2,)), dma((1,))]
     scratch += [dma((5,)), dma((1,)), dma((1,)), dma((1,)), dma((1,)), dma((1,)), dma((5,)), dma((3,))]
     embedding, grads = pl.pallas_call(

time: 79.1 us -> 77.2 us (0.976)
  Pallas kernels: 78.3 us -> 76.4 us
    pallas_call x1, Pallas kernels: 75.2 us -> 73.3 us  [shards(): pl.pallas_call(functools.partial(kernel, 1.0 / math.sqrt(nodes)), out_sha...]
where the time goes in v4:
time: 77.2 us; the launch traced here: 77.1 us
  Pallas kernels  76.4 us (99%)
    pallas_call x1, Pallas kernels, shards(): pl.pallas_call(functools.partial(kernel, 1.0 / math.sqrt(nodes)), out_sha...  73.3 us
    pallas_call x1, Pallas kernels, shards(): pl.pallas_call(finish, out_shape=(jax.ShapeDtypeStruct(block, BF16), jax....  3.14 us

profile of v4, /device:TPU:1, one launch (start us, length us, event | category | flops | bytes accessed | tf_op | source)
XLA Modules:
  0.0 77.1 jit_solution(14615825880984914204)
XLA Ops:
  0.6 73.3 %graph_step.1 = (bf16[128,256]{1,0:T(8,128)(2,1)}, bf16[2,16,16,512]{3,2,1,0:T(8,128)(2,1)}) custom-call(s32[4,16]{1,0:T(4,128)} %bitcast.2, s32[1,16]{1,0:T(1,128)} %bitcast.3, bf16[128,256]{1,0:T(8,128)(2,1)} %x_hbm.1, bf16[16,4,128,128]{3,2,1,0:T(8,128)(2,1)} %adj_hbm.1, bf16[256,512]{1,0:T(8,128)(2,1)} %w1_hbm.1, bf16[512,256]{1,0:T(8,128)(2,1)} %w2_hbm.1, ...), custom_call_target="tpu_custom_call" | custom-call | tf_op jit(solution)/shard_map/graph_step/pallas_call | solution.py:666
  73.9 3.1 %finish.1 = (bf16[128,256]{1,0:T(8,128)(2,1)}, f32[256,512]{1,0:T(8,128)}, f32[512,256]{1,0:T(8,128)}) custom-call(bf16[128,256]{1,0:T(8,128)(2,1)} %get-tuple-element.5.emb_in, bf16[2,16,16,512]{3,2,1,0:T(8,128)(2,1)} %get-tuple-element.6.g_in), custom_call_target="tpu_custom_call" | custom-call | tf_op jit(solution)/shard_map/finish/pallas_call | solution.py:680

commit v5 on v4

--- a/solution.py
+++ b/solution.py
@@ -172,7 +172,6 @@
     greet(barrier)
     emb_out = pltpu.make_async_copy(emb_s, emb_hbm, s_out.at[0])
     g_own_out = pltpu.make_async_copy(gfin.at[core], g_hbm.at[core], s_out.at[1])
-    g_sib_out = pltpu.make_async_copy(gfin.at[1 - core], g_hbm.at[1 - core], s_out.at[2])
     fetch = [
         pltpu.make_async_copy(src, dst, s_in.at[i])
         for i, (src, dst) in enumerate(
@@ -491,14 +490,12 @@
 
     def g_core():
         wait(gplane_r, ra_g.at[0])
-        send(gfin.at[core], gfin.at[core], s_g.at[4], rf_g.at[0], sib)
+        send(gfin.at[core], g_hbm.at[core], s_g.at[4], rf_g.at[0], sib)
         g_own_out.start()
 
     def g_out():
-        wait(gfin.at[1 - core], rf_g.at[0])
-        g_sib_out.start()
+        wait(g_hbm.at[1 - core], rf_g.at[0])
         g_own_out.wait()
-        g_sib_out.wait()
 
     def g_sent():
         wait(gsib, s_g.at[0])
@@ -507,18 +504,19 @@
         wait(gplane_r, s_g.at[3])
         wait(gfin.at[0], s_g.at[4])
 
+    greeted(barrier)
+    gather_start(x_hbm, feat1, s_ag1, r_ag1, f_ag1)
+    greet(near2)
     cot_turn()
-    greeted(barrier)
-    greet(near2)
-    gather_start(x_hbm, feat1, s_ag1, r_ag1, f_ag1)
     cot_z(1)
     cot_z(3)
     cot_y(0)
     fetch[2].wait()
-    loop(0, rep // 2, densify)
+    loop(0, rep // 4, densify)
     greeted(near2)
+    cot_z(2)
     greet(near3)
-    cot_z(2)
+    loop(rep // 4, rep // 2, densify)
     gather_pass(feat1, s_ag1, r_ag1, f_ag1, [0])
     cot_y(1)
     cot_y(3)

time: 77.2 us -> 76.7 us (level)
  no operation moved by 1% of the time
where the time goes in v5:
time: 76.7 us; the launch traced here: 76.6 us
  Pallas kernels  75.9 us (99%)
    pallas_call x1, Pallas kernels, shards(): pl.pallas_call(functools.partial(kernel, 1.0 / math.sqrt(nodes)), out_sha...  72.8 us
    pallas_call x1, Pallas kernels, shards(): pl.pallas_call(finish, out_shape=(jax.ShapeDtypeStruct(block, BF16), jax....  3.14 us

profile of v5, /device:TPU:1, one launch (start us, length us, event | category | flops | bytes accessed | tf_op | source)
XLA Modules:
  0.0 76.6 jit_solution(9977754215725888376)
XLA Ops:
  0.6 72.8 %graph_step.1 = (bf16[128,256]{1,0:T(8,128)(2,1)}, bf16[2,16,16,512]{3,2,1,0:T(8,128)(2,1)}) custom-call(s32[4,16]{1,0:T(4,128)} %bitcast.2, s32[1,16]{1,0:T(1,128)} %bitcast.3, bf16[128,256]{1,0:T(8,128)(2,1)} %x_hbm.1, bf16[16,4,128,128]{3,2,1,0:T(8,128)(2,1)} %adj_hbm.1, bf16[256,512]{1,0:T(8,128)(2,1)} %w1_hbm.1, bf16[512,256]{1,0:T(8,128)(2,1)} %w2_hbm.1, ...), custom_call_target="tpu_custom_call" | custom-call | tf_op jit(solution)/shard_map/graph_step/pallas_call | solution.py:664
  73.4 3.1 %finish.1 = (bf16[128,256]{1,0:T(8,128)(2,1)}, f32[256,512]{1,0:T(8,128)}, f32[512,256]{1,0:T(8,128)}) custom-call(bf16[128,256]{1,0:T(8,128)(2,1)} %get-tuple-element.5.emb_in, bf16[2,16,16,512]{3,2,1,0:T(8,128)(2,1)} %get-tuple-element.6.g_in), custom_call_target="tpu_custom_call" | custom-call | tf_op jit(solution)/shard_map/finish/pallas_call | solution.py:678

commit v6 on v5

--- a/solution.py
+++ b/solution.py
@@ -557,9 +557,9 @@
     second_start()
     g_line()
     second_fold(0)
+    g_gather()
     second_fold(1)
     second_tail()
-    g_gather()
     second_fold(2)
     second_fold(3)
     g_core()

time: 76.7 us -> 76.6 us (level)
  no operation moved by 1% of the time
where the time goes in v6:
time: 76.6 us; the launch traced here: 76.4 us
  Pallas kernels  75.8 us (99%)
    pallas_call x1, Pallas kernels, shards(): pl.pallas_call(functools.partial(kernel, 1.0 / math.sqrt(nodes)), out_sha...  72.7 us
    pallas_call x1, Pallas kernels, shards(): pl.pallas_call(finish, out_shape=(jax.ShapeDtypeStruct(block, BF16), jax....  3.14 us

profile of v6, /device:TPU:1, one launch (start us, length us, event | category | flops | bytes accessed | tf_op | source)
XLA Modules:
  0.0 76.4 jit_solution(10044557321076625236)
XLA Ops:
  0.6 72.7 %graph_step.1 = (bf16[128,256]{1,0:T(8,128)(2,1)}, bf16[2,16,16,512]{3,2,1,0:T(8,128)(2,1)}) custom-call(s32[4,16]{1,0:T(4,128)} %bitcast.2, s32[1,16]{1,0:T(1,128)} %bitcast.3, bf16[128,256]{1,0:T(8,128)(2,1)} %x_hbm.1, bf16[16,4,128,128]{3,2,1,0:T(8,128)(2,1)} %adj_hbm.1, bf16[256,512]{1,0:T(8,128)(2,1)} %w1_hbm.1, bf16[512,256]{1,0:T(8,128)(2,1)} %w2_hbm.1, ...), custom_call_target="tpu_custom_call" | custom-call | tf_op jit(solution)/shard_map/graph_step/pallas_call | solution.py:664
  73.3 3.1 %finish.1 = (bf16[128,256]{1,0:T(8,128)(2,1)}, f32[256,512]{1,0:T(8,128)}, f32[512,256]{1,0:T(8,128)}) custom-call(bf16[128,256]{1,0:T(8,128)(2,1)} %get-tuple-element.5.emb_in, bf16[2,16,16,512]{3,2,1,0:T(8,128)(2,1)} %get-tuple-element.6.g_in), custom_call_target="tpu_custom_call" | custom-call | tf_op jit(solution)/shard_map/finish/pallas_call | solution.py:678
